TPU v7x, 32 devices: a whole 2x2x4 slice. The times are simulated.
32 devices in a mesh: row: 8 (over z, y), col: 4 (over x, core).
Axes of the slice: x: 2, y: 2, z: 4, core: 2. Of those that a mesh axis runs over, the one named last changes fastest.
Arguments:
- raw: int32 [8192, 4096], P('col', 'row'), may hold values from -128 to 127
- taps: int32 [16, 128], replicated, may hold values from -256 to 256
Outputs:
- visibility: bfloat16 [32, 4096, 2, 4096], P(None, 'row', None, 'col')
All inputs are finite; a program needn't handle non-finite values.
Results may differ from a plain program's by a relative error of at most 0.0056.
Values may be sent and summed in bfloat16 or wider, within the bound.
No kernel may reach another device: no remote copies, remote signals or barrier semaphores. Data moves between devices by JAX's collectives and lax.ppermute only.
A program may use at most 384 MiB of HBM per device.

v0:
```python
import math

import jax
import jax.numpy as jnp
from jax import lax
from jax.sharding import PartitionSpec as P

CHANNELS = 32
TRANSFORM = 128
TAPS = 16
SPECTRA_DEV = 16
BLOCKS = 2
CHUNKS = 4


def from_behind(block, axis, distance):
    devices = range(lax.axis_size(axis))
    route = [(i - distance, i) for i in devices if i - distance in devices]
    return lax.ppermute(block, axis, route)


def from_root(value, axis, root):
    mine = lax.axis_index(axis) == root
    return lax.psum(jnp.where(mine, value, jnp.zeros_like(value)), axis)


def dft_table():
    sample = jnp.arange(TRANSFORM, dtype=jnp.int32)[:, None]
    channel = jnp.arange(1, CHANNELS + 1, dtype=jnp.int32)[None, :]
    phase = (sample * channel % TRANSFORM).astype(jnp.float32) * (2.0 * math.pi / TRANSFORM)
    return jnp.concatenate([jnp.cos(phase), -jnp.sin(phase)], axis=1)


def channelize(extended, taps, count):
    coeffs = taps.astype(jnp.float32)
    weighted = jnp.zeros((count, TRANSFORM, extended.shape[2]), jnp.float32)
    for offset in range(TAPS):
        start = TAPS - 1 - offset
        weighted = weighted + coeffs[offset][None, :, None] * extended[
            start : start + count
        ].astype(jnp.float32)
    scale = 1.0 / (8192.0 * math.sqrt(TAPS * TRANSFORM))
    spectra = (
        jnp.einsum("sni,nk->ksi", weighted, dft_table(), precision=lax.Precision.HIGHEST) * scale
    )
    return spectra.reshape(2, CHANNELS, count, extended.shape[2]).astype(jnp.bfloat16)


def extend(raw):
    frames = raw.astype(jnp.bfloat16).reshape(SPECTRA_DEV, TRANSFORM, raw.shape[1])
    rim_frames = frames[SPECTRA_DEV - (TAPS - 1) :]
    earlier = from_behind(rim_frames, "col", 1)
    return jnp.concatenate([earlier, frames], axis=0)


def correlate(row_block, column_block):
    spectra_all = row_block.shape[2]
    left = jnp.concatenate([row_block[0], row_block[1]], axis=1)
    real_part, imag_part = column_block[0], column_block[1]
    right = jnp.concatenate(
        [
            jnp.concatenate([real_part, imag_part], axis=1),
            jnp.concatenate([-imag_part, real_part], axis=1),
        ],
        axis=2,
    )
    total = lax.dot_general(
        left, right, (((1,), (1,)), ((0,), (0,))), preferred_element_type=jnp.float32
    )
    result = (total * (1.0 / spectra_all)).astype(jnp.bfloat16)
    return result.reshape(CHANNELS, row_block.shape[3], 2, column_block.shape[3])


def general_body(raw, taps):
    pieces = channelize(extend(raw), taps, SPECTRA_DEV)
    row_block = lax.all_gather(pieces, "col", axis=2, tiled=True)
    ratio = lax.axis_size("row") // lax.axis_size("col")
    first_root = lax.axis_index("col") * ratio
    received = []
    for offset in range(ratio):
        received.append(from_root(row_block, "row", first_root + offset))
    column_block = jnp.concatenate(received, axis=3)
    return correlate(row_block, column_block)


def correlate_planes(row_part, low, high, spectra_all):
    pieces, count, depth, width = row_part.shape
    half = depth // 2

    def stacked(part):
        return jnp.transpose(part, (1, 0, 2, 3)).reshape(count, pieces * depth, width)

    def turn(part):
        return jnp.concatenate([-part[:, :, half:], part[:, :, :half]], axis=2)

    left = stacked(row_part)
    blocks = [stacked(low), stacked(high), stacked(turn(low)), stacked(turn(high))]
    right = jnp.concatenate(blocks, axis=2)
    total = lax.dot_general(
        left, right, (((1,), (1,)), ((0,), (0,))), preferred_element_type=jnp.float32
    )
    result = (total * (1.0 / spectra_all)).astype(jnp.bfloat16)
    return result.reshape(count, width, 2, 2 * width)


def device(z, y, c):
    return (z * 2 + y) * 4 + c


def routes():
    everywhere = [(z, y, c) for z in range(4) for y in range(2) for c in range(4)]
    core = [(device(z, y, c), device(z, y, c ^ 1)) for z, y, c in everywhere]
    across = [(device(z, y, c), device(z, y, c ^ 2)) for z, y, c in everywhere]
    other = [(device(z, y, c), device(z, 1 - y, c)) for z, y, c in everywhere]
    hops = [
        {0: [(0, 1)], 1: [(1, 2)], 2: [(2, 1)], 3: [(3, 2)]},
        {0: [(1, 2)], 1: [(2, 3), (1, 0)], 2: [(1, 0), (2, 3)], 3: [(2, 1)]},
        {0: [(2, 3)], 3: [(1, 0)]},
    ]
    chain = [
        [
            (device(a, y, c), device(b, y, c))
            for c, pairs in hop.items()
            for a, b in pairs
            for y in range(2)
        ]
        for hop in hops
    ]
    return core, across, other, chain


def arrival(z, c):
    away = jnp.abs(z - c)
    late = ((c == 1) & (z != 2)) | ((c == 2) & (z != 1))
    return jnp.where(away == 0, 0, jnp.where(late, 2, away))


def plane_body(raw, taps):
    core, across, other, chain = routes()
    axes = ("row", "col")
    row, col = lax.axis_index("row"), lax.axis_index("col")
    z, y = row // 2, row % 2
    hop = arrival(z, col)
    pieces = channelize(extend(raw), taps, SPECTRA_DEV)
    width = pieces.shape[3]
    own = jnp.transpose(pieces, (1, 0, 2, 3)).reshape(CHANNELS, 2 * SPECTRA_DEV, width)
    count = CHANNELS // CHUNKS
    spectra_all = SPECTRA_DEV * lax.axis_size("col")
    row_parts, lows, highs = [], [], []
    for chunk in range(CHUNKS):
        mine = own[chunk * count : (chunk + 1) * count]
        opposite = lax.ppermute(mine, axes, across)
        pair = jnp.stack([mine, opposite])
        row_part = jnp.concatenate([pair, lax.ppermute(pair, axes, core)], axis=0)
        first = lax.ppermute(row_part, axes, chain[0])
        held = jnp.where(hop == 0, row_part, first)
        second = lax.ppermute(held, axes, chain[1])
        held = jnp.where(hop == 2, second, held)
        third = lax.ppermute(second, axes, chain[2])
        near = jnp.where(hop == 3, third, held)
        far = lax.ppermute(near, axes, other)
        row_parts.append(row_part)
        lows.append(jnp.where(y == 0, near, far))
        highs.append(jnp.where(y == 0, far, near))
    operands = [jnp.concatenate(parts, axis=1) for parts in (row_parts, lows, highs)]
    return correlate_planes(*operands, spectra_all)


def solution(mesh):
    planes = mesh.shape["row"] == 8 and mesh.shape["col"] == 4
    placed = (P("col", "row"), P())
    return jax.shard_map(
        plane_body if planes else general_body,
        mesh=mesh,
        in_specs=placed,
        out_specs=P(None, "row", None, "col"),
        check_vma=False,
    )
```

profile of v0, /device:TPU:17, one launch (start us, length us, event | category | flops | bytes accessed | tf_op | source)
XLA Modules:
  0.0 416.2 jit_solution(6571849437009289740)
XLA Ops:
  0.0 2.8 convert_element_type.70
  2.9 3.7 collective-permute-start
  6.8 21.3 %collective-permute-done = bf16[15,128,512]{2,1,0:T(8,128)(2,1)S(1)} collective-permute-done((bf16[15,128,512]{2,1,0:T(8,128)(2,1)S(1)}, bf16[15,128,512]{2,1,0:T(8,128)(2,1)S(1)}, u32[]{:S(2)}, u32[]{:S(2)}) %collective-permute-start) | collective-permute-done | bytes 1966112 | tf_op jit(solution)/shard_map/ppermute | solution.py:19
  28.2 10.8 %multiply_convert_fusion.1 = bf16[64,16,512]{2,0,1:T(8,128)(2,1)S(1)} fusion(bf16[16,128,512]{2,1,0:T(8,128)(2,1)S(1)} %bitcast.70, bf16[15,128,512]{2,1,0:T(8,128)(2,1)S(1)} %collective-permute-done, f32[128]{0:T(128)S(1)} %get-tuple-element.26, f32[128]{0:T(128)S(1)} %get-tuple-element.27, f32[128]{0:T(128)S(1)} %get-tuple-element.28, ...), kind=kOutput, calls=%fused_computation.107 | convolution fusion | flops 902832128 | bytes 5152768 | tf_op jit(solution)/shard_map/sni,nk->ksi/dot_general | solution.py:44
  41.1 5.5 %collective-permute-done.3 = bf16[8,32,512]{2,1,0:T(8,128)(2,1)S(1)} collective-permute-done((bf16[8,32,512]{2,1,0:T(8,128)(2,1)S(1)}, bf16[8,32,512]{2,1,0:T(8,128)(2,1)S(1)}, u32[]{:S(2)}, u32[]{:S(2)}) %collective-permute-start.3) | collective-permute-done | bytes 262176 | tf_op jit(solution)/shard_map/ppermute | solution.py:152
  46.7 3.2 collective-permute-start.4
  52.3 2.8 collective-permute-start.6
  55.1 3.2 collective-permute-done.7
  58.3 2.4 collective-permute-start.8
  72.8 4.9 %collective-permute-done.13 = bf16[4,8,32,512]{3,2,1,0:T(8,128)(2,1)} collective-permute-done((bf16[4,8,32,512]{3,2,1,0:T(8,128)(2,1)}, bf16[4,8,32,512]{3,2,1,0:T(8,128)(2,1)}, u32[]{:S(2)}, u32[]{:S(2)}) %collective-permute-start.13) | collective-permute-done | bytes 1048608 | tf_op jit(solution)/shard_map/ppermute | solution.py:155
  79.0 2.3 collective-permute-start.14
  81.3 13.8 %collective-permute-done.17 = bf16[4,8,32,512]{3,2,1,0:T(8,128)(2,1)} collective-permute-done((bf16[4,8,32,512]{3,2,1,0:T(8,128)(2,1)}, bf16[4,8,32,512]{3,2,1,0:T(8,128)(2,1)}, u32[]{:S(2)}, u32[]{:S(2)}) %collective-permute-start.17) | collective-permute-done | bytes 1048608 | tf_op jit(solution)/shard_map/ppermute | solution.py:155
  96.5 2.3 collective-permute-start.18
  98.8 18.8 %collective-permute-done.21 = bf16[4,8,32,512]{3,2,1,0:T(8,128)(2,1)} collective-permute-done((bf16[4,8,32,512]{3,2,1,0:T(8,128)(2,1)}, bf16[4,8,32,512]{3,2,1,0:T(8,128)(2,1)}, u32[]{:S(2)}, u32[]{:S(2)}) %collective-permute-start.21) | collective-permute-done | bytes 1048608 | tf_op jit(solution)/shard_map/ppermute | solution.py:155
  119.0 2.3 collective-permute-start.22
  121.2 18.8 %collective-permute-done.9 = bf16[4,8,32,512]{3,2,1,0:T(8,128)(2,1)} collective-permute-done((bf16[4,8,32,512]{3,2,1,0:T(8,128)(2,1)}, bf16[4,8,32,512]{3,2,1,0:T(8,128)(2,1)}, u32[]{:S(2)}, u32[]{:S(2)}) %collective-permute-start.9) | collective-permute-done | bytes 1048608 | tf_op jit(solution)/shard_map/ppermute | solution.py:155
  142.4 2.3 collective-permute-start.10
  146.3 1.6 collective-permute-start.19
  149.6 13.3 %collective-permute-done.10 = bf16[4,8,32,512]{3,2,1,0:T(8,128)(2,1)} collective-permute-done((bf16[4,8,32,512]{3,2,1,0:T(8,128)(2,1)S(1)}, bf16[4,8,32,512]{3,2,1,0:T(8,128)(2,1)}, u32[]{:S(2)}, u32[]{:S(2)}) %collective-permute-start.10) | collective-permute-done | bytes 1048608 | tf_op jit(solution)/shard_map/ppermute | solution.py:157
  162.9 1.7 collective-permute-start.11
  170.5 2.5 copy.5
  173.0 18.4 %collective-permute-done.16 = bf16[4,8,32,512]{3,2,1,0:T(8,128)(2,1)S(1)} collective-permute-done((bf16[4,8,32,512]{3,2,1,0:T(8,128)(2,1)S(1)}, bf16[4,8,32,512]{3,2,1,0:T(8,128)(2,1)S(1)}, u32[]{:S(2)}, u32[]{:S(2)}) %collective-permute-start.16) | collective-permute-done | bytes 1048608 | tf_op jit(solution)/shard_map/ppermute | solution.py:161
  192.6 21.4 %collective-permute-done.20 = bf16[4,8,32,512]{3,2,1,0:T(8,128)(2,1)S(1)} collective-permute-done((bf16[4,8,32,512]{3,2,1,0:T(8,128)(2,1)S(1)}, bf16[4,8,32,512]{3,2,1,0:T(8,128)(2,1)S(1)}, u32[]{:S(2)}, u32[]{:S(2)}) %collective-permute-start.20) | collective-permute-done | bytes 1048608 | tf_op jit(solution)/shard_map/ppermute | solution.py:161
  215.5 20.9 %collective-permute-done.24 = bf16[4,8,32,512]{3,2,1,0:T(8,128)(2,1)S(1)} collective-permute-done((bf16[4,8,32,512]{3,2,1,0:T(8,128)(2,1)S(1)}, bf16[4,8,32,512]{3,2,1,0:T(8,128)(2,1)S(1)}, u32[]{:S(2)}, u32[]{:S(2)}) %collective-permute-start.24) | collective-permute-done | bytes 1048608 | tf_op jit(solution)/shard_map/ppermute | solution.py:161
  237.9 15.8 %collective-permute-done.12 = bf16[4,8,32,512]{3,2,1,0:T(8,128)(2,1)S(1)} collective-permute-done((bf16[4,8,32,512]{3,2,1,0:T(8,128)(2,1)S(1)}, bf16[4,8,32,512]{3,2,1,0:T(8,128)(2,1)S(1)}, u32[]{:S(2)}, u32[]{:S(2)}) %collective-permute-start.12) | collective-permute-done | bytes 1048608 | tf_op jit(solution)/shard_map/ppermute | solution.py:161
  255.1 5.1 %fusion.114 = (bf16[32,4,32,512]{3,2,0,1:T(8,128)(2,1)}, bf16[4,32,32,512]{3,2,1,0:T(8,128)(2,1)S(1)}, bf16[4,32,32,512]{3,2,1,0:T(8,128)(2,1)S(1)}, bf16[32,4,32,512]{3,2,0,1:T(8,128)(2,1)S(1)}) fusion(bf16[4,8,32,512]{3,2,1,0:T(8,128)(2,1)} %get-tuple-element.20, bf16[4,8,32,512]{3,2,1,0:T(8,128)(2,1)} %get-tuple-element.18, ...), kind=kLoop, calls=%fused_computation.183 | loop fusion | flops 12582912 | bytes 25165824 | tf_op jit(solution)/shard_map/transpose | solution.py:91
  260.2 4.7 %copy.7 = bf16[32,4,32,512]{3,2,1,0:T(8,128)(2,1)} copy(bf16[32,4,32,512]{3,2,0,1:T(8,128)(2,1)} %get-tuple-element.7) | data formatting | bytes 8388608 | tf_op jit(solution)/shard_map/transpose | solution.py:91
  265.0 2.3 copy.6
  267.9 2.6 copy.9
  271.2 2.7 copy.8
  273.9 35.0 %multiply_convert_fusion = bf16[32,512,2048]{2,1,0:T(8,128)(2,1)} fusion(bf16[32,128,512]{2,1,0:T(8,128)(2,1)} %bitcast.91, bf16[32,128,512]{2,1,0:T(8,128)(2,1)} %bitcast.94, bf16[32,128,512]{2,1,0:T(8,128)(2,1)} %bitcast.95, bf16[32,128,512]{2,1,0:T(8,128)(2,1)} %bitcast.92, bf16[32,128,512]{2,1,0:T(8,128)(2,1)} %bitcast.93), kind=kOutput, calls=%fused_computation | convolution fusion | flops 8724152320 | bytes 88080384 | tf_op jit(solution)/shard_map/dot_general | solution.py:99
  308.9 107.3 %reshape.59 = bf16[32,512,2,1024]{3,2,1,0:T(2,128)(2,1)} reshape(bf16[32,512,2048]{2,1,0:T(8,128)(2,1)} %multiply_convert_fusion) | data formatting | bytes 134217728 | tf_op jit(solution)/shard_map/reshape | solution.py:103
  (92 shorter events, 39.6 us)
Async XLA Ops:
  2.9 25.2 %collective-permute-start = (bf16[15,128,512]{2,1,0:T(8,128)(2,1)S(1)}, bf16[15,128,512]{2,1,0:T(8,128)(2,1)S(1)}, u32[]{:S(2)}, u32[]{:S(2)}) collective-permute-start(bf16[15,128,512]{2,1,0:T(8,128)(2,1)S(1)} %bitcast.113), channel_id=1, source_target_pairs={{0,1},{1,2},{2,3},{4,5},{5,6},{6,7},{8,9},{9,10},{10,11},{12,13},{... | collective-permute-start | bytes 5898248 | tf_op jit(solution)/shard_map/ppermute | solution.py:19
  39.6 7.0 %collective-permute-start.3 = (bf16[8,32,512]{2,1,0:T(8,128)(2,1)S(1)}, bf16[8,32,512]{2,1,0:T(8,128)(2,1)S(1)}, u32[]{:S(2)}, u32[]{:S(2)}) collective-permute-start(bf16[8,32,512]{2,1,0:T(8,128)(2,1)S(1)} %bitcast.86), channel_id=1, source_target_pairs={{0,2},{1,3},{2,0},{3,1},{4,6},{5,7},{6,4},{7,5},{8,10},{9,11},{10,... | collective-permute-start | bytes 786440 | tf_op jit(solution)/shard_map/ppermute | solution.py:152
  39.7 12.6 %collective-permute-start.5 = (bf16[8,32,512]{2,1,0:T(8,128)(2,1)S(1)}, bf16[8,32,512]{2,1,0:T(8,128)(2,1)S(1)}, u32[]{:S(2)}, u32[]{:S(2)}) collective-permute-start(bf16[8,32,512]{2,1,0:T(8,128)(2,1)S(1)} %bitcast.81), channel_id=1, source_target_pairs={{0,2},{1,3},{2,0},{3,1},{4,6},{5,7},{6,4},{7,5},{8,10},{9,11},{10,... | collective-permute-start | bytes 786440 | tf_op jit(solution)/shard_map/ppermute | solution.py:152
  46.7 14.0 %collective-permute-start.4 = (bf16[2,8,32,512]{3,2,1,0:T(8,128)(2,1)S(1)}, bf16[2,8,32,512]{3,2,1,0:T(8,128)(2,1)S(1)}, u32[]{:S(2)}, u32[]{:S(2)}) collective-permute-start(bf16[2,8,32,512]{3,2,1,0:T(8,128)(2,1)S(1)} %pad_maximum_fusion.9), channel_id=1, source_target_pairs={{0,1},{1,0},{2,3},{3,2},{4,5},{5,4},{6,7},{7,6},{8,9},{9,8},{10,11... | collective-permute-start | bytes 1572872 | tf_op jit(solution)/shard_map/ppermute | solution.py:154
  49.9 8.4 %collective-permute-start.7 = (bf16[8,32,512]{2,1,0:T(8,128)(2,1)S(1)}, bf16[8,32,512]{2,1,0:T(8,128)(2,1)S(1)}, u32[]{:S(2)}, u32[]{:S(2)}) collective-permute-start(bf16[8,32,512]{2,1,0:T(8,128)(2,1)S(1)} %bitcast.76), channel_id=1, source_target_pairs={{0,2},{1,3},{2,0},{3,1},{4,6},{5,7},{6,4},{7,5},{8,10},{9,11},{10,... | collective-permute-start | bytes 786440 | tf_op jit(solution)/shard_map/ppermute | solution.py:152
  52.3 16.8 %copy-start.7 = (bf16[8,32,512]{2,1,0:T(8,128)(2,1)}, bf16[8,32,512]{2,1,0:T(8,128)(2,1)S(1)}, u32[]{:S(2)}) copy-start(bf16[8,32,512]{2,1,0:T(8,128)(2,1)S(1)} %collective-permute-done.5) | copy-start | bytes 786436
  52.3 13.1 %collective-permute-start.6 = (bf16[2,8,32,512]{3,2,1,0:T(8,128)(2,1)S(1)}, bf16[2,8,32,512]{3,2,1,0:T(8,128)(2,1)S(1)}, u32[]{:S(2)}, u32[]{:S(2)}) collective-permute-start(bf16[2,8,32,512]{3,2,1,0:T(8,128)(2,1)S(1)} %pad_maximum_fusion.10), channel_id=1, source_target_pairs={{0,1},{1,0},{2,3},{3,2},{4,5},{5,4},{6,7},{7,6},{8,9},{9,8},{10,11... | collective-permute-start | bytes 1572872 | tf_op jit(solution)/shard_map/ppermute | solution.py:154
  55.1 8.8 %collective-permute-start.1 = (bf16[8,32,512]{2,1,0:T(8,128)(2,1)S(1)}, bf16[8,32,512]{2,1,0:T(8,128)(2,1)S(1)}, u32[]{:S(2)}, u32[]{:S(2)}) collective-permute-start(bf16[8,32,512]{2,1,0:T(8,128)(2,1)S(1)} %bitcast.71), channel_id=1, source_target_pairs={{0,2},{1,3},{2,0},{3,1},{4,6},{5,7},{6,4},{7,5},{8,10},{9,11},{10,... | collective-permute-start | bytes 786440 | tf_op jit(solution)/shard_map/ppermute | solution.py:152
  58.3 10.7 %copy-start.9 = (bf16[8,32,512]{2,1,0:T(8,128)(2,1)}, bf16[8,32,512]{2,1,0:T(8,128)(2,1)S(1)}, u32[]{:S(2)}) copy-start(bf16[8,32,512]{2,1,0:T(8,128)(2,1)S(1)} %collective-permute-done.7) | copy-start | bytes 786436
  58.3 9.6 %collective-permute-start.8 = (bf16[2,8,32,512]{3,2,1,0:T(8,128)(2,1)S(1)}, bf16[2,8,32,512]{3,2,1,0:T(8,128)(2,1)S(1)}, u32[]{:S(2)}, u32[]{:S(2)}) collective-permute-start(bf16[2,8,32,512]{3,2,1,0:T(8,128)(2,1)S(1)} %pad_maximum_fusion.11), channel_id=1, source_target_pairs={{0,1},{1,0},{2,3},{3,2},{4,5},{5,4},{6,7},{7,6},{8,9},{9,8},{10,11... | collective-permute-start | bytes 1572872 | tf_op jit(solution)/shard_map/ppermute | solution.py:154
  61.8 15.8 %collective-permute-start.13 = (bf16[4,8,32,512]{3,2,1,0:T(8,128)(2,1)}, bf16[4,8,32,512]{3,2,1,0:T(8,128)(2,1)}, u32[]{:S(2)}, u32[]{:S(2)}) collective-permute-start(bf16[4,8,32,512]{3,2,1,0:T(8,128)(2,1)} %pad_maximum_fusion.5), channel_id=1, source_target_pairs={{0,8},{4,12},{9,17},{13,21},{18,10},{22,14},{27,19},{31,23}} | collective-permute-start | bytes 3145736 | tf_op jit(solution)/shard_map/ppermute | solution.py:155
  63.9 6.4 %collective-permute-start.2 = (bf16[2,8,32,512]{3,2,1,0:T(8,128)(2,1)S(1)}, bf16[2,8,32,512]{3,2,1,0:T(8,128)(2,1)S(1)}, u32[]{:S(2)}, u32[]{:S(2)}) collective-permute-start(bf16[2,8,32,512]{3,2,1,0:T(8,128)(2,1)S(1)} %pad_maximum_fusion.8), channel_id=1, source_target_pairs={{0,1},{1,0},{2,3},{3,2},{4,5},{5,4},{6,7},{7,6},{8,9},{9,8},{10,11... | collective-permute-start | bytes 1572872 | tf_op jit(solution)/shard_map/ppermute | solution.py:154
  66.5 28.7 %collective-permute-start.17 = (bf16[4,8,32,512]{3,2,1,0:T(8,128)(2,1)}, bf16[4,8,32,512]{3,2,1,0:T(8,128)(2,1)}, u32[]{:S(2)}, u32[]{:S(2)}) collective-permute-start(bf16[4,8,32,512]{3,2,1,0:T(8,128)(2,1)} %pad_maximum_fusion.6), channel_id=1, source_target_pairs={{0,8},{4,12},{9,17},{13,21},{18,10},{22,14},{27,19},{31,23}} | collective-permute-start | bytes 3145736 | tf_op jit(solution)/shard_map/ppermute | solution.py:155
  69.0 48.6 %collective-permute-start.21 = (bf16[4,8,32,512]{3,2,1,0:T(8,128)(2,1)}, bf16[4,8,32,512]{3,2,1,0:T(8,128)(2,1)}, u32[]{:S(2)}, u32[]{:S(2)}) collective-permute-start(bf16[4,8,32,512]{3,2,1,0:T(8,128)(2,1)} %pad_maximum_fusion.7), channel_id=1, source_target_pairs={{0,8},{4,12},{9,17},{13,21},{18,10},{22,14},{27,19},{31,23}} | collective-permute-start | bytes 3145736 | tf_op jit(solution)/shard_map/ppermute | solution.py:155
  71.4 68.6 %collective-permute-start.9 = (bf16[4,8,32,512]{3,2,1,0:T(8,128)(2,1)}, bf16[4,8,32,512]{3,2,1,0:T(8,128)(2,1)}, u32[]{:S(2)}, u32[]{:S(2)}) collective-permute-start(bf16[4,8,32,512]{3,2,1,0:T(8,128)(2,1)} %pad_maximum_fusion.4), channel_id=1, source_target_pairs={{0,8},{4,12},{9,17},{13,21},{18,10},{22,14},{27,19},{31,23}} | collective-permute-start | bytes 3145736 | tf_op jit(solution)/shard_map/ppermute | solution.py:155
  72.7 44.9 %copy-start.10 = (bf16[8,32,512]{2,1,0:T(8,128)(2,1)S(1)}, bf16[8,32,512]{2,1,0:T(8,128)(2,1)}, u32[]{:S(2)}) copy-start(bf16[8,32,512]{2,1,0:T(8,128)(2,1)} %copy-done.9) | copy-start | bytes 786436
  72.8 67.3 %copy-start.13 = (bf16[8,32,512]{2,1,0:T(8,128)(2,1)S(1)}, bf16[8,32,512]{2,1,0:T(8,128)(2,1)}, u32[]{:S(2)}) copy-start(bf16[8,32,512]{2,1,0:T(8,128)(2,1)} %copy-done.12) | copy-start | bytes 786436
  79.0 62.4 %copy-start.6 = (bf16[4,8,32,512]{3,2,1,0:T(8,128)(2,1)}, bf16[4,8,32,512]{3,2,1,0:T(8,128)(2,1)S(1)}, u32[]{:S(2)}) copy-start(bf16[4,8,32,512]{3,2,1,0:T(8,128)(2,1)S(1)} %broadcast_select_fusion.2) | copy-start | bytes 3145732
  79.0 65.7 %collective-permute-start.14 = (bf16[4,8,32,512]{3,2,1,0:T(8,128)(2,1)S(1)}, bf16[4,8,32,512]{3,2,1,0:T(8,128)(2,1)}, u32[]{:S(2)}, u32[]{:S(2)}) collective-permute-start(bf16[4,8,32,512]{3,2,1,0:T(8,128)(2,1)S(1)} %broadcast_select_fusion.2), channel_id=1, source_target_pairs={{8,16},{12,20},{17,25},{21,29},{9,1},{13,5},{10,2},{14,6},{18,26},... | collective-permute-start | bytes 3145736 | tf_op jit(solution)/shard_map/ppermute | solution.py:157
  96.5 66.4 %copy-start.4 = (bf16[4,8,32,512]{3,2,1,0:T(8,128)(2,1)}, bf16[4,8,32,512]{3,2,1,0:T(8,128)(2,1)S(1)}, u32[]{:S(2)}) copy-start(bf16[4,8,32,512]{3,2,1,0:T(8,128)(2,1)S(1)} %broadcast_select_fusion.1) | copy-start | bytes 3145732
  96.5 49.8 %collective-permute-start.18 = (bf16[4,8,32,512]{3,2,1,0:T(8,128)(2,1)S(1)}, bf16[4,8,32,512]{3,2,1,0:T(8,128)(2,1)}, u32[]{:S(2)}, u32[]{:S(2)}) collective-permute-start(bf16[4,8,32,512]{3,2,1,0:T(8,128)(2,1)S(1)} %broadcast_select_fusion.1), channel_id=1, source_target_pairs={{8,16},{12,20},{17,25},{21,29},{9,1},{13,5},{10,2},{14,6},{18,26},... | collective-permute-start | bytes 3145736 | tf_op jit(solution)/shard_map/ppermute | solution.py:157
  119.0 43.9 %copy-start.2 = (bf16[4,8,32,512]{3,2,1,0:T(8,128)(2,1)}, bf16[4,8,32,512]{3,2,1,0:T(8,128)(2,1)S(1)}, u32[]{:S(2)}) copy-start(bf16[4,8,32,512]{3,2,1,0:T(8,128)(2,1)S(1)} %broadcast_select_fusion) | copy-start | bytes 3145732
  119.0 29.0 %collective-permute-start.22 = (bf16[4,8,32,512]{3,2,1,0:T(8,128)(2,1)S(1)}, bf16[4,8,32,512]{3,2,1,0:T(8,128)(2,1)}, u32[]{:S(2)}, u32[]{:S(2)}) collective-permute-start(bf16[4,8,32,512]{3,2,1,0:T(8,128)(2,1)S(1)} %broadcast_select_fusion), channel_id=1, source_target_pairs={{8,16},{12,20},{17,25},{21,29},{9,1},{13,5},{10,2},{14,6},{18,26},... | collective-permute-start | bytes 3145736 | tf_op jit(solution)/shard_map/ppermute | solution.py:157
  142.4 20.5 %collective-permute-start.10 = (bf16[4,8,32,512]{3,2,1,0:T(8,128)(2,1)S(1)}, bf16[4,8,32,512]{3,2,1,0:T(8,128)(2,1)}, u32[]{:S(2)}, u32[]{:S(2)}) collective-permute-start(bf16[4,8,32,512]{3,2,1,0:T(8,128)(2,1)S(1)} %broadcast_select_fusion.3), channel_id=1, source_target_pairs={{8,16},{12,20},{17,25},{21,29},{9,1},{13,5},{10,2},{14,6},{18,26},... | collective-permute-start | bytes 3145736 | tf_op jit(solution)/shard_map/ppermute | solution.py:157
  144.7 19.9 %collective-permute-start.15 = (bf16[4,8,32,512]{3,2,1,0:T(8,128)(2,1)}, bf16[4,8,32,512]{3,2,1,0:T(8,128)(2,1)}, u32[]{:S(2)}, u32[]{:S(2)}) collective-permute-start(bf16[4,8,32,512]{3,2,1,0:T(8,128)(2,1)} %collective-permute-done.14), channel_id=1, source_target_pairs={{16,24},{20,28},{11,3},{15,7}} | collective-permute-start | bytes 3145736 | tf_op jit(solution)/shard_map/ppermute | solution.py:159
  146.3 21.1 %collective-permute-start.19 = (bf16[4,8,32,512]{3,2,1,0:T(8,128)(2,1)}, bf16[4,8,32,512]{3,2,1,0:T(8,128)(2,1)}, u32[]{:S(2)}, u32[]{:S(2)}) collective-permute-start(bf16[4,8,32,512]{3,2,1,0:T(8,128)(2,1)} %collective-permute-done.18), channel_id=1, source_target_pairs={{16,24},{20,28},{11,3},{15,7}} | collective-permute-start | bytes 3145736 | tf_op jit(solution)/shard_map/ppermute | solution.py:159
  148.0 20.0 %collective-permute-start.23 = (bf16[4,8,32,512]{3,2,1,0:T(8,128)(2,1)}, bf16[4,8,32,512]{3,2,1,0:T(8,128)(2,1)}, u32[]{:S(2)}, u32[]{:S(2)}) collective-permute-start(bf16[4,8,32,512]{3,2,1,0:T(8,128)(2,1)} %collective-permute-done.22), channel_id=1, source_target_pairs={{16,24},{20,28},{11,3},{15,7}} | collective-permute-start | bytes 3145736 | tf_op jit(solution)/shard_map/ppermute | solution.py:159
  162.9 6.5 %collective-permute-start.11 = (bf16[4,8,32,512]{3,2,1,0:T(8,128)(2,1)}, bf16[4,8,32,512]{3,2,1,0:T(8,128)(2,1)}, u32[]{:S(2)}, u32[]{:S(2)}) collective-permute-start(bf16[4,8,32,512]{3,2,1,0:T(8,128)(2,1)} %collective-permute-done.10), channel_id=1, source_target_pairs={{16,24},{20,28},{11,3},{15,7}} | collective-permute-start | bytes 3145736 | tf_op jit(solution)/shard_map/ppermute | solution.py:159
  166.1 25.3 %collective-permute-start.16 = (bf16[4,8,32,512]{3,2,1,0:T(8,128)(2,1)S(1)}, bf16[4,8,32,512]{3,2,1,0:T(8,128)(2,1)S(1)}, u32[]{:S(2)}, u32[]{:S(2)}) collective-permute-start(bf16[4,8,32,512]{3,2,1,0:T(8,128)(2,1)S(1)} %select_select_fusion.2), channel_id=1, source_target_pairs={{0,4},{1,5},{2,6},{3,7},{4,0},{5,1},{6,2},{7,3},{8,12},{9,13},{10,... | collective-permute-start | bytes 3145736 | tf_op jit(solution)/shard_map/ppermute | solution.py:161
  167.6 46.3 %collective-permute-start.20 = (bf16[4,8,32,512]{3,2,1,0:T(8,128)(2,1)S(1)}, bf16[4,8,32,512]{3,2,1,0:T(8,128)(2,1)S(1)}, u32[]{:S(2)}, u32[]{:S(2)}) collective-permute-start(bf16[4,8,32,512]{3,2,1,0:T(8,128)(2,1)S(1)} %select_select_fusion.1), channel_id=1, source_target_pairs={{0,4},{1,5},{2,6},{3,7},{4,0},{5,1},{6,2},{7,3},{8,12},{9,13},{10,... | collective-permute-start | bytes 3145736 | tf_op jit(solution)/shard_map/ppermute | solution.py:161
  168.1 68.3 %collective-permute-start.24 = (bf16[4,8,32,512]{3,2,1,0:T(8,128)(2,1)S(1)}, bf16[4,8,32,512]{3,2,1,0:T(8,128)(2,1)S(1)}, u32[]{:S(2)}, u32[]{:S(2)}) collective-permute-start(bf16[4,8,32,512]{3,2,1,0:T(8,128)(2,1)S(1)} %select_select_fusion), channel_id=1, source_target_pairs={{0,4},{1,5},{2,6},{3,7},{4,0},{5,1},{6,2},{7,3},{8,12},{9,13},{10,... | collective-permute-start | bytes 3145736 | tf_op jit(solution)/shard_map/ppermute | solution.py:161
  169.6 84.1 %collective-permute-start.12 = (bf16[4,8,32,512]{3,2,1,0:T(8,128)(2,1)S(1)}, bf16[4,8,32,512]{3,2,1,0:T(8,128)(2,1)S(1)}, u32[]{:S(2)}, u32[]{:S(2)}) collective-permute-start(bf16[4,8,32,512]{3,2,1,0:T(8,128)(2,1)S(1)} %select_select_fusion.3), channel_id=1, source_target_pairs={{0,4},{1,5},{2,6},{3,7},{4,0},{5,1},{6,2},{7,3},{8,12},{9,13},{10,... | collective-permute-start | bytes 3145736 | tf_op jit(solution)/shard_map/ppermute | solution.py:161
  (9 other events, 30.2 us)
where the time goes:
time: 420 us; the launch traced here: 416 us
  waiting for transfers between devices  178 us (42%)
  local copies, waits for them, and re-layouts  124 us (30%)
  matrix products  45.8 us (11%)
  starting transfers between devices  40.6 us (10%)
  other arithmetic  27.7 us (7%)
    reshape x1, local copies, waits for them, and re-layouts, correlate_planes(): return result.reshape(count, width, 2, 2 * width)  107 us
    ppermute x4, waiting for transfers between devices, plane_body(): far = lax.ppermute(near, axes, other)  76.5 us
    ppermute x4, waiting for transfers between devices, plane_body(): first = lax.ppermute(row_part, axes, chain[0])  56.3 us
    dot_general x1, matrix products, correlate_planes(): lax.dot_general(left, right, (((1,), (1,)), ((0,), (0,))), preferred_elem...  35 us
    ppermute x1, waiting for transfers between devices, from_behind(): return lax.ppermute(block, axis, route)  21.3 us
    transpose x5, local copies, waits for them, and re-layouts, stacked(): jnp.transpose(part, (1, 0, 2, 3)).reshape(count, pieces * depth, width)  14.8 us
    ppermute x4, waiting for transfers between devices, plane_body(): second = lax.ppermute(held, axes, chain[1])  13.3 us
    dot_general x1, matrix products, channelize(): jnp.einsum('sni,nk->ksi', weighted, dft_table(), precision=lax.Precision....  10.8 us
  transfers between devices with their start and end apart: 25, of which 14 were waited for; matrix products, arithmetic and copies ran while one was open for 5% of the time, Pallas kernels for 0%

commit v1 on v0

--- a/solution.py
+++ b/solution.py
@@ -147,19 +147,27 @@
     count = CHANNELS // CHUNKS
     spectra_all = SPECTRA_DEV * lax.axis_size("col")
     row_parts, lows, highs = [], [], []
+    arrived, fars = [], []
     for chunk in range(CHUNKS):
         mine = own[chunk * count : (chunk + 1) * count]
         opposite = lax.ppermute(mine, axes, across)
         pair = jnp.stack([mine, opposite])
         row_part = jnp.concatenate([pair, lax.ppermute(pair, axes, core)], axis=0)
+        if chunk >= 2:
+            row_part, arrived[-2] = lax.optimization_barrier((row_part, arrived[-2]))
         first = lax.ppermute(row_part, axes, chain[0])
         held = jnp.where(hop == 0, row_part, first)
+        if chunk >= 2:
+            held, fars[-2] = lax.optimization_barrier((held, fars[-2]))
         second = lax.ppermute(held, axes, chain[1])
         held = jnp.where(hop == 2, second, held)
         third = lax.ppermute(second, axes, chain[2])
         near = jnp.where(hop == 3, third, held)
+        arrived.append(near)
         far = lax.ppermute(near, axes, other)
         row_parts.append(row_part)
+        fars.append(far)
+    for near, far in zip(arrived, fars):
         lows.append(jnp.where(y == 0, near, far))
         highs.append(jnp.where(y == 0, far, near))
     operands = [jnp.concatenate(parts, axis=1) for parts in (row_parts, lows, highs)]

time: 420 us -> 413 us (0.983)
  the two profiles are of different devices: /device:TPU:17 before, /device:TPU:6 now
where the time goes in v1:
time: 413 us; the launch traced here: 409 us
  waiting for transfers between devices  163 us (39%)
  local copies, waits for them, and re-layouts  124 us (30%)
  starting transfers between devices  46.3 us (11%)
  matrix products  45.9 us (11%)
  other arithmetic  30.2 us (7%)
    reshape x1, local copies, waits for them, and re-layouts, correlate_planes(): return result.reshape(count, width, 2, 2 * width)  107 us
    ppermute x4, waiting for transfers between devices, plane_body(): far = lax.ppermute(near, axes, other)  75.6 us
    ppermute x4, waiting for transfers between devices, plane_body(): second = lax.ppermute(held, axes, chain[1])  52.6 us
    dot_general x1, matrix products, correlate_planes(): lax.dot_general(left, right, (((1,), (1,)), ((0,), (0,))), preferred_elem...  35.1 us
    ppermute x1, waiting for transfers between devices, from_behind(): return lax.ppermute(block, axis, route)  23.8 us
    ppermute x4, starting transfers between devices, plane_body(): opposite = lax.ppermute(mine, axes, across)  23.1 us
    transpose x5, local copies, waits for them, and re-layouts, stacked(): jnp.transpose(part, (1, 0, 2, 3)).reshape(count, pieces * depth, width)  14.9 us
    dot_general x1, matrix products, channelize(): jnp.einsum('sni,nk->ksi', weighted, dft_table(), precision=lax.Precision....  10.8 us
  transfers between devices with their start and end apart: 25, of which 11 were waited for; matrix products, arithmetic and copies ran while one was open for 5% of the time, Pallas kernels for 0%

profile of v1, /device:TPU:6, one launch (start us, length us, event | category | flops | bytes accessed | tf_op | source)
XLA Modules:
  0.0 409.3 jit_solution(11769269112465234813)
XLA Ops:
  0.0 2.8 convert_element_type.70
  2.9 1.9 collective-permute-start
  5.0 23.8 %collective-permute-done = bf16[15,128,512]{2,1,0:T(8,128)(2,1)S(1)} collective-permute-done((bf16[15,128,512]{2,1,0:T(8,128)(2,1)S(1)}, bf16[15,128,512]{2,1,0:T(8,128)(2,1)S(1)}, u32[]{:S(2)}, u32[]{:S(2)}) %collective-permute-start) | collective-permute-done | bytes 1966112 | tf_op jit(solution)/shard_map/ppermute | solution.py:19
  28.9 10.8 %multiply_convert_fusion.1 = bf16[64,16,512]{2,0,1:T(8,128)(2,1)S(1)} fusion(bf16[16,128,512]{2,1,0:T(8,128)(2,1)S(1)} %bitcast.70, bf16[15,128,512]{2,1,0:T(8,128)(2,1)S(1)} %collective-permute-done, f32[128]{0:T(128)S(1)} %get-tuple-element.42, f32[128]{0:T(128)S(1)} %get-tuple-element.43, f32[128]{0:T(128)S(1)} %get-tuple-element.44, ...), kind=kOutput, calls=%fused_computation.107 | convolution fusion | flops 902832128 | bytes 5152768 | tf_op jit(solution)/shard_map/sni,nk->ksi/dot_general | solution.py:44
  40.4 2.0 collective-permute-start.1
  42.4 6.9 %collective-permute-done.3 = bf16[8,32,512]{2,1,0:T(8,128)(2,1)S(1)} collective-permute-done((bf16[8,32,512]{2,1,0:T(8,128)(2,1)S(1)}, bf16[8,32,512]{2,1,0:T(8,128)(2,1)S(1)}, u32[]{:S(2)}, u32[]{:S(2)}) %collective-permute-start.3) | collective-permute-done | bytes 262176 | tf_op jit(solution)/shard_map/ppermute | solution.py:153
  49.5 2.7 collective-permute-done.1
  53.4 1.7 collective-permute-start.12
  56.2 1.6 collective-permute-start.7
  63.4 21.0 %collective-permute-start.5 = (bf16[8,32,512]{2,1,0:T(8,128)(2,1)S(1)}, bf16[8,32,512]{2,1,0:T(8,128)(2,1)S(1)}, u32[]{:S(2)}, u32[]{:S(2)}) collective-permute-start(bf16[8,32,512]{2,1,0:T(8,128)(2,1)S(1)} %bitcast.98), channel_id=1, source_target_pairs={{0,2},{1,3},{2,0},{3,1},{4,6},{5,7},{6,4},{7,5},{8,10},{9,11},{10,... | collective-permute-start | bytes 786440 | tf_op jit(solution)/shard_map/ppermute | solution.py:153
  84.5 3.0 collective-permute-done.13
  87.5 1.7 collective-permute-start.14
  89.3 24.7 %collective-permute-done.8 = bf16[4,8,32,512]{3,2,1,0:T(8,128)(2,1)} collective-permute-done((bf16[4,8,32,512]{3,2,1,0:T(8,128)(2,1)S(1)}, bf16[4,8,32,512]{3,2,1,0:T(8,128)(2,1)}, u32[]{:S(2)}, u32[]{:S(2)}) %collective-permute-start.8) | collective-permute-done | bytes 1048608 | tf_op jit(solution)/shard_map/ppermute | solution.py:162
  114.0 1.6 collective-permute-start.9
  124.9 1.6 collective-permute-start.16
  126.7 20.9 %collective-permute-done.18 = bf16[4,8,32,512]{3,2,1,0:T(8,128)(2,1)S(1)} collective-permute-done((bf16[4,8,32,512]{3,2,1,0:T(8,128)(2,1)S(1)}, bf16[4,8,32,512]{3,2,1,0:T(8,128)(2,1)S(1)}, u32[]{:S(2)}, u32[]{:S(2)}) %collective-permute-start.18) | collective-permute-done | bytes 1048608 | tf_op jit(solution)/shard_map/ppermute | solution.py:167
  149.0 20.2 %collective-permute-done.16 = bf16[4,8,32,512]{3,2,1,0:T(8,128)(2,1)S(1)} collective-permute-done((bf16[4,8,32,512]{3,2,1,0:T(8,128)(2,1)S(1)}, bf16[4,8,32,512]{3,2,1,0:T(8,128)(2,1)S(1)}, u32[]{:S(2)}, u32[]{:S(2)}) %collective-permute-start.16) | collective-permute-done | bytes 1048608 | tf_op jit(solution)/shard_map/ppermute | solution.py:167
  170.5 1.6 collective-permute-start.23
  172.2 24.9 %collective-permute-done.19 = bf16[4,8,32,512]{3,2,1,0:T(8,128)(2,1)} collective-permute-done((bf16[4,8,32,512]{3,2,1,0:T(8,128)(2,1)S(1)}, bf16[4,8,32,512]{3,2,1,0:T(8,128)(2,1)}, u32[]{:S(2)}, u32[]{:S(2)}) %collective-permute-start.19) | collective-permute-done | bytes 1048608 | tf_op jit(solution)/shard_map/ppermute | solution.py:162
  197.1 1.7 collective-permute-start.20
  202.4 1.6 collective-permute-start.21
  204.6 2.5 copy.5
  210.5 16.0 %collective-permute-done.24 = bf16[4,8,32,512]{3,2,1,0:T(8,128)(2,1)S(1)} collective-permute-done((bf16[4,8,32,512]{3,2,1,0:T(8,128)(2,1)S(1)}, bf16[4,8,32,512]{3,2,1,0:T(8,128)(2,1)S(1)}, u32[]{:S(2)}, u32[]{:S(2)}) %collective-permute-start.24) | collective-permute-done | bytes 1048608 | tf_op jit(solution)/shard_map/ppermute | solution.py:167
  227.9 18.5 %collective-permute-done.21 = bf16[4,8,32,512]{3,2,1,0:T(8,128)(2,1)S(1)} collective-permute-done((bf16[4,8,32,512]{3,2,1,0:T(8,128)(2,1)S(1)}, bf16[4,8,32,512]{3,2,1,0:T(8,128)(2,1)S(1)}, u32[]{:S(2)}, u32[]{:S(2)}) %collective-permute-start.21) | collective-permute-done | bytes 1048608 | tf_op jit(solution)/shard_map/ppermute | solution.py:167
  246.5 1.5 broadcast_select_fusion.5
  248.0 5.1 %fusion.114 = (bf16[32,4,32,512]{3,2,0,1:T(8,128)(2,1)}, bf16[4,32,32,512]{3,2,1,0:T(8,128)(2,1)S(1)}, bf16[4,32,32,512]{3,2,1,0:T(8,128)(2,1)S(1)}, bf16[32,4,32,512]{3,2,0,1:T(8,128)(2,1)S(1)}) fusion(bf16[4,8,32,512]{3,2,1,0:T(8,128)(2,1)} %get-tuple-element.36, bf16[4,8,32,512]{3,2,1,0:T(8,128)(2,1)} %get-tuple-element.34, ...), kind=kLoop, calls=%fused_computation.183 | loop fusion | flops 12582912 | bytes 25165824 | tf_op jit(solution)/shard_map/transpose | solution.py:91
  253.1 4.8 %copy.7 = bf16[32,4,32,512]{3,2,1,0:T(8,128)(2,1)} copy(bf16[32,4,32,512]{3,2,0,1:T(8,128)(2,1)} %get-tuple-element.23) | data formatting | bytes 8388608 | tf_op jit(solution)/shard_map/transpose | solution.py:91
  257.9 2.3 copy.6
  260.9 2.6 copy.9
  264.2 2.7 copy.8
  266.9 35.1 %multiply_convert_fusion = bf16[32,512,2048]{2,1,0:T(8,128)(2,1)} fusion(bf16[32,128,512]{2,1,0:T(8,128)(2,1)} %bitcast.81, bf16[32,128,512]{2,1,0:T(8,128)(2,1)} %bitcast.84, bf16[32,128,512]{2,1,0:T(8,128)(2,1)} %bitcast.85, bf16[32,128,512]{2,1,0:T(8,128)(2,1)} %bitcast.82, bf16[32,128,512]{2,1,0:T(8,128)(2,1)} %bitcast.83), kind=kOutput, calls=%fused_computation | convolution fusion | flops 8724152320 | bytes 88080384 | tf_op jit(solution)/shard_map/dot_general | solution.py:99
  302.0 107.3 %reshape.59 = bf16[32,512,2,1024]{3,2,1,0:T(2,128)(2,1)} reshape(bf16[32,512,2048]{2,1,0:T(8,128)(2,1)} %multiply_convert_fusion) | data formatting | bytes 134217728 | tf_op jit(solution)/shard_map/reshape | solution.py:103
  (104 shorter events, 31.7 us)
Async XLA Ops:
  2.9 25.9 %collective-permute-start = (bf16[15,128,512]{2,1,0:T(8,128)(2,1)S(1)}, bf16[15,128,512]{2,1,0:T(8,128)(2,1)S(1)}, u32[]{:S(2)}, u32[]{:S(2)}) collective-permute-start(bf16[15,128,512]{2,1,0:T(8,128)(2,1)S(1)} %bitcast.101), channel_id=1, source_target_pairs={{0,1},{1,2},{2,3},{4,5},{5,6},{6,7},{8,9},{9,10},{10,11},{12,13},{... | collective-permute-start | bytes 5898248 | tf_op jit(solution)/shard_map/ppermute | solution.py:19
  40.3 75.3 %copy-start.15 = (bf16[8,2,16,512]{3,2,1,0:T(8,128)(2,1)}, bf16[8,2,16,512]{3,2,1,0:T(8,128)(2,1)S(1)}, u32[]{:S(2)}) copy-start(bf16[8,2,16,512]{3,2,1,0:T(8,128)(2,1)S(1)} %get-tuple-element.38) | copy-start | bytes 786436
  40.3 9.0 %collective-permute-start.3 = (bf16[8,32,512]{2,1,0:T(8,128)(2,1)S(1)}, bf16[8,32,512]{2,1,0:T(8,128)(2,1)S(1)}, u32[]{:S(2)}, u32[]{:S(2)}) collective-permute-start(bf16[8,32,512]{2,1,0:T(8,128)(2,1)S(1)} %bitcast.76), channel_id=1, source_target_pairs={{0,2},{1,3},{2,0},{3,1},{4,6},{5,7},{6,4},{7,5},{8,10},{9,11},{10,... | collective-permute-start | bytes 786440 | tf_op jit(solution)/shard_map/ppermute | solution.py:153
  40.4 11.7 %collective-permute-start.1 = (bf16[8,32,512]{2,1,0:T(8,128)(2,1)S(1)}, bf16[8,32,512]{2,1,0:T(8,128)(2,1)S(1)}, u32[]{:S(2)}, u32[]{:S(2)}) collective-permute-start(bf16[8,32,512]{2,1,0:T(8,128)(2,1)S(1)} %bitcast.71), channel_id=1, source_target_pairs={{0,2},{1,3},{2,0},{3,1},{4,6},{5,7},{6,4},{7,5},{8,10},{9,11},{10,... | collective-permute-start | bytes 786440 | tf_op jit(solution)/shard_map/ppermute | solution.py:153
  49.4 2.9 collective-permute-start.4
  52.2 2.8 collective-permute-start.2
  53.4 4.5 %collective-permute-start.12 = (bf16[4,8,32,512]{3,2,1,0:T(8,128)(2,1)}, bf16[4,8,32,512]{3,2,1,0:T(8,128)(2,1)}, u32[]{:S(2)}, u32[]{:S(2)}) collective-permute-start(bf16[4,8,32,512]{3,2,1,0:T(8,128)(2,1)} %pad_maximum_fusion.5), channel_id=1, source_target_pairs={{0,8},{4,12},{9,17},{13,21},{18,10},{22,14},{27,19},{31,23}} | collective-permute-start | bytes 3145736 | tf_op jit(solution)/shard_map/ppermute | solution.py:158
  56.2 4.3 %collective-permute-start.7 = (bf16[4,8,32,512]{3,2,1,0:T(8,128)(2,1)}, bf16[4,8,32,512]{3,2,1,0:T(8,128)(2,1)}, u32[]{:S(2)}, u32[]{:S(2)}) collective-permute-start(bf16[4,8,32,512]{3,2,1,0:T(8,128)(2,1)} %pad_maximum_fusion.4), channel_id=1, source_target_pairs={{0,8},{4,12},{9,17},{13,21},{18,10},{22,14},{27,19},{31,23}} | collective-permute-start | bytes 3145736 | tf_op jit(solution)/shard_map/ppermute | solution.py:158
  59.2 54.8 %copy-start.8 = (bf16[4,8,32,512]{3,2,1,0:T(8,128)(2,1)}, bf16[4,8,32,512]{3,2,1,0:T(8,128)(2,1)S(1)}, u32[]{:S(2)}) copy-start(bf16[4,8,32,512]{3,2,1,0:T(8,128)(2,1)S(1)} %broadcast_select_fusion.10) | copy-start | bytes 3145732
  59.2 28.3 %collective-permute-start.13 = (bf16[4,8,32,512]{3,2,1,0:T(8,128)(2,1)S(1)}, bf16[4,8,32,512]{3,2,1,0:T(8,128)(2,1)}, u32[]{:S(2)}, u32[]{:S(2)}) collective-permute-start(bf16[4,8,32,512]{3,2,1,0:T(8,128)(2,1)S(1)} %broadcast_select_fusion.10), channel_id=1, source_target_pairs={{8,16},{12,20},{17,25},{21,29},{9,1},{13,5},{10,2},{14,6},{18,26},... | collective-permute-start | bytes 3145736 | tf_op jit(solution)/shard_map/ppermute | solution.py:162
  61.9 52.1 %collective-permute-start.8 = (bf16[4,8,32,512]{3,2,1,0:T(8,128)(2,1)S(1)}, bf16[4,8,32,512]{3,2,1,0:T(8,128)(2,1)}, u32[]{:S(2)}, u32[]{:S(2)}) collective-permute-start(bf16[4,8,32,512]{3,2,1,0:T(8,128)(2,1)S(1)} %broadcast_select_fusion.11), channel_id=1, source_target_pairs={{8,16},{12,20},{17,25},{21,29},{9,1},{13,5},{10,2},{14,6},{18,26},... | collective-permute-start | bytes 3145736 | tf_op jit(solution)/shard_map/ppermute | solution.py:162
  63.4 25.7 %collective-permute-start.5 = (bf16[8,32,512]{2,1,0:T(8,128)(2,1)S(1)}, bf16[8,32,512]{2,1,0:T(8,128)(2,1)S(1)}, u32[]{:S(2)}, u32[]{:S(2)}) collective-permute-start(bf16[8,32,512]{2,1,0:T(8,128)(2,1)S(1)} %bitcast.98), channel_id=1, source_target_pairs={{0,2},{1,3},{2,0},{3,1},{4,6},{5,7},{6,4},{7,5},{8,10},{9,11},{10,... | collective-permute-start | bytes 786440 | tf_op jit(solution)/shard_map/ppermute | solution.py:153
  84.4 31.2 %collective-permute-start.10 = (bf16[8,32,512]{2,1,0:T(8,128)(2,1)S(1)}, bf16[8,32,512]{2,1,0:T(8,128)(2,1)S(1)}, u32[]{:S(2)}, u32[]{:S(2)}) collective-permute-start(bf16[8,32,512]{2,1,0:T(8,128)(2,1)S(1)} %bitcast.95), channel_id=1, source_target_pairs={{0,2},{1,3},{2,0},{3,1},{4,6},{5,7},{6,4},{7,5},{8,10},{9,11},{10,... | collective-permute-start | bytes 786440 | tf_op jit(solution)/shard_map/ppermute | solution.py:153
  87.5 32.6 %collective-permute-start.14 = (bf16[4,8,32,512]{3,2,1,0:T(8,128)(2,1)}, bf16[4,8,32,512]{3,2,1,0:T(8,128)(2,1)}, u32[]{:S(2)}, u32[]{:S(2)}) collective-permute-start(bf16[4,8,32,512]{3,2,1,0:T(8,128)(2,1)} %collective-permute-done.13), channel_id=1, source_target_pairs={{16,24},{20,28},{11,3},{15,7}} | collective-permute-start | bytes 3145736 | tf_op jit(solution)/shard_map/ppermute | solution.py:164
  89.2 27.3 %collective-permute-start.6 = (bf16[2,8,32,512]{3,2,1,0:T(8,128)(2,1)S(1)}, bf16[2,8,32,512]{3,2,1,0:T(8,128)(2,1)}, u32[]{:S(2)}, u32[]{:S(2)}) collective-permute-start(bf16[2,8,32,512]{3,2,1,0:T(8,128)(2,1)S(1)} %pad_maximum_fusion.10), channel_id=1, source_target_pairs={{0,1},{1,0},{2,3},{3,2},{4,5},{5,4},{6,7},{7,6},{8,9},{9,8},{10,11... | collective-permute-start | bytes 1572872 | tf_op jit(solution)/shard_map/ppermute | solution.py:155
  114.0 8.8 %collective-permute-start.9 = (bf16[4,8,32,512]{3,2,1,0:T(8,128)(2,1)}, bf16[4,8,32,512]{3,2,1,0:T(8,128)(2,1)}, u32[]{:S(2)}, u32[]{:S(2)}) collective-permute-start(bf16[4,8,32,512]{3,2,1,0:T(8,128)(2,1)} %collective-permute-done.8), channel_id=1, source_target_pairs={{16,24},{20,28},{11,3},{15,7}} | collective-permute-start | bytes 3145736 | tf_op jit(solution)/shard_map/ppermute | solution.py:164
  116.5 2.3 collective-permute-start.11
  121.5 27.5 %copy-start.2 = (bf16[4,8,32,512]{3,2,1,0:T(8,128)(2,1)}, bf16[4,8,32,512]{3,2,1,0:T(8,128)(2,1)S(1)}, u32[]{:S(2)}) copy-start(bf16[4,8,32,512]{3,2,1,0:T(8,128)(2,1)S(1)} %select_select_fusion.2) | copy-start | bytes 3145732
  121.5 26.1 %collective-permute-start.18 = (bf16[4,8,32,512]{3,2,1,0:T(8,128)(2,1)S(1)}, bf16[4,8,32,512]{3,2,1,0:T(8,128)(2,1)S(1)}, u32[]{:S(2)}, u32[]{:S(2)}) collective-permute-start(bf16[4,8,32,512]{3,2,1,0:T(8,128)(2,1)S(1)} %select_select_fusion.2), channel_id=1, source_target_pairs={{0,4},{1,5},{2,6},{3,7},{4,0},{5,1},{6,2},{7,3},{8,12},{9,13},{10,... | collective-permute-start | bytes 3145736 | tf_op jit(solution)/shard_map/ppermute | solution.py:167
  122.0 4.5 %collective-permute-start.17 = (bf16[4,8,32,512]{3,2,1,0:T(8,128)(2,1)S(1)}, bf16[4,8,32,512]{3,2,1,0:T(8,128)(2,1)S(1)}, u32[]{:S(2)}, u32[]{:S(2)}) collective-permute-start(bf16[4,8,32,512]{3,2,1,0:T(8,128)(2,1)S(1)} %pad_maximum_fusion.7), channel_id=1, source_target_pairs={{0,8},{4,12},{9,17},{13,21},{18,10},{22,14},{27,19},{31,23}} | collective-permute-start | bytes 3145736 | tf_op jit(solution)/shard_map/ppermute | solution.py:158
  124.2 45.0 %copy-start.4 = (bf16[4,8,32,512]{3,2,1,0:T(8,128)(2,1)}, bf16[4,8,32,512]{3,2,1,0:T(8,128)(2,1)S(1)}, u32[]{:S(2)}) copy-start(bf16[4,8,32,512]{3,2,1,0:T(8,128)(2,1)S(1)} %select_select_fusion.3) | copy-start | bytes 3145732
  124.2 24.7 %collective-permute-start.15 = (bf16[4,8,32,512]{3,2,1,0:T(8,128)(2,1)S(1)}, bf16[4,8,32,512]{3,2,1,0:T(8,128)(2,1)S(1)}, u32[]{:S(2)}, u32[]{:S(2)}) collective-permute-start(bf16[4,8,32,512]{3,2,1,0:T(8,128)(2,1)S(1)} %pad_maximum_fusion.6), channel_id=1, source_target_pairs={{0,8},{4,12},{9,17},{13,21},{18,10},{22,14},{27,19},{31,23}} | collective-permute-start | bytes 3145736 | tf_op jit(solution)/shard_map/ppermute | solution.py:158
  124.9 44.3 %collective-permute-start.16 = (bf16[4,8,32,512]{3,2,1,0:T(8,128)(2,1)S(1)}, bf16[4,8,32,512]{3,2,1,0:T(8,128)(2,1)S(1)}, u32[]{:S(2)}, u32[]{:S(2)}) collective-permute-start(bf16[4,8,32,512]{3,2,1,0:T(8,128)(2,1)S(1)} %select_select_fusion.3), channel_id=1, source_target_pairs={{0,4},{1,5},{2,6},{3,7},{4,0},{5,1},{6,2},{7,3},{8,12},{9,13},{10,... | collective-permute-start | bytes 3145736 | tf_op jit(solution)/shard_map/ppermute | solution.py:167
  126.7 70.4 %copy-start.12 = (bf16[4,8,32,512]{3,2,1,0:T(8,128)(2,1)}, bf16[4,8,32,512]{3,2,1,0:T(8,128)(2,1)S(1)}, u32[]{:S(2)}) copy-start(bf16[4,8,32,512]{3,2,1,0:T(8,128)(2,1)S(1)} %broadcast_select_fusion.8) | copy-start | bytes 3145732
  147.5 49.5 %copy-start.16 = (bf16[4,8,32,512]{3,2,1,0:T(8,128)(2,1)}, bf16[4,8,32,512]{3,2,1,0:T(8,128)(2,1)S(1)}, u32[]{:S(2)}) copy-start(bf16[4,8,32,512]{3,2,1,0:T(8,128)(2,1)S(1)} %collective-permute-done.18) | copy-start | bytes 3145732
  147.6 23.0 %collective-permute-start.22 = (bf16[4,8,32,512]{3,2,1,0:T(8,128)(2,1)S(1)}, bf16[4,8,32,512]{3,2,1,0:T(8,128)(2,1)}, u32[]{:S(2)}, u32[]{:S(2)}) collective-permute-start(bf16[4,8,32,512]{3,2,1,0:T(8,128)(2,1)S(1)} %broadcast_select_fusion.8), channel_id=1, source_target_pairs={{8,16},{12,20},{17,25},{21,29},{9,1},{13,5},{10,2},{14,6},{18,26},... | collective-permute-start | bytes 3145736 | tf_op jit(solution)/shard_map/ppermute | solution.py:162
  169.2 27.8 %copy-start.18 = (bf16[4,8,32,512]{3,2,1,0:T(8,128)(2,1)}, bf16[4,8,32,512]{3,2,1,0:T(8,128)(2,1)S(1)}, u32[]{:S(2)}) copy-start(bf16[4,8,32,512]{3,2,1,0:T(8,128)(2,1)S(1)} %collective-permute-done.16) | copy-start | bytes 3145732
  169.2 27.8 %collective-permute-start.19 = (bf16[4,8,32,512]{3,2,1,0:T(8,128)(2,1)S(1)}, bf16[4,8,32,512]{3,2,1,0:T(8,128)(2,1)}, u32[]{:S(2)}, u32[]{:S(2)}) collective-permute-start(bf16[4,8,32,512]{3,2,1,0:T(8,128)(2,1)S(1)} %broadcast_select_fusion.9), channel_id=1, source_target_pairs={{8,16},{12,20},{17,25},{21,29},{9,1},{13,5},{10,2},{14,6},{18,26},... | collective-permute-start | bytes 3145736 | tf_op jit(solution)/shard_map/ppermute | solution.py:162
  170.5 28.3 %collective-permute-start.23 = (bf16[4,8,32,512]{3,2,1,0:T(8,128)(2,1)}, bf16[4,8,32,512]{3,2,1,0:T(8,128)(2,1)}, u32[]{:S(2)}, u32[]{:S(2)}) collective-permute-start(bf16[4,8,32,512]{3,2,1,0:T(8,128)(2,1)} %collective-permute-done.22), channel_id=1, source_target_pairs={{16,24},{20,28},{11,3},{15,7}} | collective-permute-start | bytes 3145736 | tf_op jit(solution)/shard_map/ppermute | solution.py:164
  197.1 3.8 collective-permute-start.20
  200.3 26.2 %collective-permute-start.24 = (bf16[4,8,32,512]{3,2,1,0:T(8,128)(2,1)S(1)}, bf16[4,8,32,512]{3,2,1,0:T(8,128)(2,1)S(1)}, u32[]{:S(2)}, u32[]{:S(2)}) collective-permute-start(bf16[4,8,32,512]{3,2,1,0:T(8,128)(2,1)S(1)} %select_select_fusion), channel_id=1, source_target_pairs={{0,4},{1,5},{2,6},{3,7},{4,0},{5,1},{6,2},{7,3},{8,12},{9,13},{10,... | collective-permute-start | bytes 3145736 | tf_op jit(solution)/shard_map/ppermute | solution.py:167
  202.4 44.1 %collective-permute-start.21 = (bf16[4,8,32,512]{3,2,1,0:T(8,128)(2,1)S(1)}, bf16[4,8,32,512]{3,2,1,0:T(8,128)(2,1)S(1)}, u32[]{:S(2)}, u32[]{:S(2)}) collective-permute-start(bf16[4,8,32,512]{3,2,1,0:T(8,128)(2,1)S(1)} %select_select_fusion.1), channel_id=1, source_target_pairs={{0,4},{1,5},{2,6},{3,7},{4,0},{5,1},{6,2},{7,3},{8,12},{9,13},{10,... | collective-permute-start | bytes 3145736 | tf_op jit(solution)/shard_map/ppermute | solution.py:167
  (15 other events, 76.2 us)

commit v2 on v1

--- a/solution.py
+++ b/solution.py
@@ -141,8 +141,9 @@
     row, col = lax.axis_index("row"), lax.axis_index("col")
     z, y = row // 2, row % 2
     hop = arrival(z, col)
-    pieces = channelize(extend(raw), taps, SPECTRA_DEV)
-    width = pieces.shape[3]
+    width = raw.shape[1]
+    sides = [extend(raw[:, : width // 2]), extend(raw[:, width // 2 :])]
+    pieces = jnp.concatenate([channelize(side, taps, SPECTRA_DEV) for side in sides], axis=3)
     own = jnp.transpose(pieces, (1, 0, 2, 3)).reshape(CHANNELS, 2 * SPECTRA_DEV, width)
     count = CHANNELS // CHUNKS
     spectra_all = SPECTRA_DEV * lax.axis_size("col")

time: 413 us -> 409 us (level)
  waiting for transfers between devices: 163 us -> 156 us
    ppermute x1 -> x2, waiting for transfers between devices: 23.8 us -> 16.4 us  [from_behind(): return lax.ppermute(block, axis, route)]
    dot_general x1 -> x2, matrix products: 10.8 us -> 10.2 us  [channelize(): jnp.einsum('sni,nk->ksi', weighted, dft_table(), precision=lax.Precision....]
  transfers between devices with their start and end apart: 25 -> 26, of which waited for: 11 -> 13; matrix products, arithmetic and copies ran while one was open for 5% -> 7% of each run, Pallas kernels for 0% -> 0%
where the time goes in v2:
time: 409 us; the launch traced here: 405 us
  waiting for transfers between devices  156 us (38%)
  local copies, waits for them, and re-layouts  125 us (31%)
  starting transfers between devices  48 us (12%)
  matrix products  45.3 us (11%)
  other arithmetic  30.3 us (7%)
    reshape x1, local copies, waits for them, and re-layouts, correlate_planes(): return result.reshape(count, width, 2, 2 * width)  107 us
    ppermute x4, waiting for transfers between devices, plane_body(): far = lax.ppermute(near, axes, other)  75.6 us
    ppermute x4, waiting for transfers between devices, plane_body(): second = lax.ppermute(held, axes, chain[1])  53.4 us
    dot_general x1, matrix products, correlate_planes(): lax.dot_general(left, right, (((1,), (1,)), ((0,), (0,))), preferred_elem...  35.1 us
    ppermute x4, starting transfers between devices, plane_body(): opposite = lax.ppermute(mine, axes, across)  22.9 us
    ppermute x2, waiting for transfers between devices, from_behind(): return lax.ppermute(block, axis, route)  16.4 us
    transpose x5, local copies, waits for them, and re-layouts, stacked(): jnp.transpose(part, (1, 0, 2, 3)).reshape(count, pieces * depth, width)  14.9 us
    dot_general x2, matrix products, channelize(): jnp.einsum('sni,nk->ksi', weighted, dft_table(), precision=lax.Precision....  10.2 us
  transfers between devices with their start and end apart: 26, of which 13 were waited for; matrix products, arithmetic and copies ran while one was open for 7% of the time, Pallas kernels for 0%

profile of v2, /device:TPU:6, one launch (start us, length us, event | category | flops | bytes accessed | tf_op | source)
XLA Modules:
  0.0 405.4 jit_solution(3767069583944232010)
XLA Ops:
  0.0 2.8 convert.4
  2.9 1.9 collective-permute-start.1
  4.8 1.9 collective-permute-start
  7.1 11.2 %collective-permute-done.1 = bf16[15,128,256]{2,1,0:T(8,128)(2,1)S(1)} collective-permute-done((bf16[15,128,256]{2,1,0:T(8,128)(2,1)S(1)}, bf16[15,128,256]{2,1,0:T(8,128)(2,1)S(1)}, u32[]{:S(2)}, u32[]{:S(2)}) %collective-permute-start.1) | collective-permute-done | bytes 983072 | tf_op jit(solution)/shard_map/ppermute | solution.py:19
  18.3 5.0 %fusion.109 = bf16[64,16,256]{2,0,1:T(8,128)(2,1)S(1)} fusion(bf16[16,128,256]{2,1,0:T(8,128)(2,1)S(1)} %bitcast.103, bf16[15,128,256]{2,1,0:T(8,128)(2,1)S(1)} %collective-permute-done.1, f32[128]{0:T(128)S(1)} %get-tuple-element.46, f32[128]{0:T(128)S(1)} %get-tuple-element.47, f32[128]{0:T(128)S(1)} %get-tuple-element.48, ...), kind=kOutput, calls=%fused_computation.169 | convolution fusion | flops 451420160 | bytes 2596864 | tf_op jit(solution)/shard_map/sni,nk->ksi/dot_general | solution.py:44
  23.7 5.2 %collective-permute-done = bf16[15,128,256]{2,1,0:T(8,128)(2,1)S(1)} collective-permute-done((bf16[15,128,256]{2,1,0:T(8,128)(2,1)S(1)}, bf16[15,128,256]{2,1,0:T(8,128)(2,1)S(1)}, u32[]{:S(2)}, u32[]{:S(2)}) %collective-permute-start) | collective-permute-done | bytes 983072 | tf_op jit(solution)/shard_map/ppermute | solution.py:19
  28.9 5.2 %fusion.112 = bf16[64,16,256]{2,0,1:T(8,128)(2,1)S(1)} fusion(bf16[16,128,256]{2,1,0:T(8,128)(2,1)S(1)} %bitcast.102, bf16[15,128,256]{2,1,0:T(8,128)(2,1)S(1)} %collective-permute-done, f32[128]{0:T(128)S(1)} %get-tuple-element.46, f32[128]{0:T(128)S(1)} %get-tuple-element.47, f32[128]{0:T(128)S(1)} %get-tuple-element.48, f32[128]{0:T(128)S(1)} %get-tuple-element.49, ...), kind=kOutput, calls=%fused_computation.170 | convolution fusion | flops 451420160 | bytes 2596864 | tf_op jit(solution)/shard_map/sni,nk->ksi/dot_general | solution.py:44
  34.6 2.0 collective-permute-start.2
  36.6 6.9 %collective-permute-done.4 = bf16[8,32,512]{2,1,0:T(8,128)(2,1)S(1)} collective-permute-done((bf16[8,32,512]{2,1,0:T(8,128)(2,1)S(1)}, bf16[8,32,512]{2,1,0:T(8,128)(2,1)S(1)}, u32[]{:S(2)}, u32[]{:S(2)}) %collective-permute-start.4) | collective-permute-done | bytes 262176 | tf_op jit(solution)/shard_map/ppermute | solution.py:154
  43.7 2.7 collective-permute-done.2
  47.6 1.7 collective-permute-start.13
  50.4 1.8 collective-permute-start.8
  58.6 20.8 %collective-permute-start.6 = (bf16[8,32,512]{2,1,0:T(8,128)(2,1)S(1)}, bf16[8,32,512]{2,1,0:T(8,128)(2,1)S(1)}, u32[]{:S(2)}, u32[]{:S(2)}) collective-permute-start(bf16[8,32,512]{2,1,0:T(8,128)(2,1)S(1)} %bitcast.99), channel_id=1, source_target_pairs={{0,2},{1,3},{2,0},{3,1},{4,6},{5,7},{6,4},{7,5},{8,10},{9,11},{10,... | collective-permute-start | bytes 786440 | tf_op jit(solution)/shard_map/ppermute | solution.py:154
  79.5 2.2 collective-permute-done.14
  81.7 1.7 collective-permute-start.15
  83.9 26.2 %collective-permute-done.9 = bf16[4,8,32,512]{3,2,1,0:T(8,128)(2,1)} collective-permute-done((bf16[4,8,32,512]{3,2,1,0:T(8,128)(2,1)S(1)}, bf16[4,8,32,512]{3,2,1,0:T(8,128)(2,1)}, u32[]{:S(2)}, u32[]{:S(2)}) %collective-permute-start.9) | collective-permute-done | bytes 1048608 | tf_op jit(solution)/shard_map/ppermute | solution.py:163
  110.1 1.6 collective-permute-start.10
  122.8 20.9 %collective-permute-done.19 = bf16[4,8,32,512]{3,2,1,0:T(8,128)(2,1)S(1)} collective-permute-done((bf16[4,8,32,512]{3,2,1,0:T(8,128)(2,1)S(1)}, bf16[4,8,32,512]{3,2,1,0:T(8,128)(2,1)S(1)}, u32[]{:S(2)}, u32[]{:S(2)}) %collective-permute-start.19) | collective-permute-done | bytes 1048608 | tf_op jit(solution)/shard_map/ppermute | solution.py:168
  145.2 20.2 %collective-permute-done.17 = bf16[4,8,32,512]{3,2,1,0:T(8,128)(2,1)S(1)} collective-permute-done((bf16[4,8,32,512]{3,2,1,0:T(8,128)(2,1)S(1)}, bf16[4,8,32,512]{3,2,1,0:T(8,128)(2,1)S(1)}, u32[]{:S(2)}, u32[]{:S(2)}) %collective-permute-start.17) | collective-permute-done | bytes 1048608 | tf_op jit(solution)/shard_map/ppermute | solution.py:168
  166.7 1.6 collective-permute-start.24
  168.3 24.9 %collective-permute-done.20 = bf16[4,8,32,512]{3,2,1,0:T(8,128)(2,1)} collective-permute-done((bf16[4,8,32,512]{3,2,1,0:T(8,128)(2,1)S(1)}, bf16[4,8,32,512]{3,2,1,0:T(8,128)(2,1)}, u32[]{:S(2)}, u32[]{:S(2)}) %collective-permute-start.20) | collective-permute-done | bytes 1048608 | tf_op jit(solution)/shard_map/ppermute | solution.py:163
  193.2 1.7 collective-permute-start.21
  200.7 2.5 copy.6
  206.6 16.0 %collective-permute-done.25 = bf16[4,8,32,512]{3,2,1,0:T(8,128)(2,1)S(1)} collective-permute-done((bf16[4,8,32,512]{3,2,1,0:T(8,128)(2,1)S(1)}, bf16[4,8,32,512]{3,2,1,0:T(8,128)(2,1)S(1)}, u32[]{:S(2)}, u32[]{:S(2)}) %collective-permute-start.25) | collective-permute-done | bytes 1048608 | tf_op jit(solution)/shard_map/ppermute | solution.py:168
  224.1 18.6 %collective-permute-done.22 = bf16[4,8,32,512]{3,2,1,0:T(8,128)(2,1)S(1)} collective-permute-done((bf16[4,8,32,512]{3,2,1,0:T(8,128)(2,1)S(1)}, bf16[4,8,32,512]{3,2,1,0:T(8,128)(2,1)S(1)}, u32[]{:S(2)}, u32[]{:S(2)}) %collective-permute-start.22) | collective-permute-done | bytes 1048608 | tf_op jit(solution)/shard_map/ppermute | solution.py:168
  244.2 5.1 %fusion.217 = (bf16[32,4,32,512]{3,2,0,1:T(8,128)(2,1)}, bf16[4,32,32,512]{3,2,1,0:T(8,128)(2,1)S(1)}, bf16[4,32,32,512]{3,2,1,0:T(8,128)(2,1)S(1)}, bf16[32,4,32,512]{3,2,0,1:T(8,128)(2,1)S(1)}) fusion(bf16[4,8,32,512]{3,2,1,0:T(8,128)(2,1)} %get-tuple-element.36, bf16[4,8,32,512]{3,2,1,0:T(8,128)(2,1)} %get-tuple-element.34, ...), kind=kLoop, calls=%fused_computation.294 | loop fusion | flops 12582912 | bytes 25165824 | tf_op jit(solution)/shard_map/transpose | solution.py:91
  249.3 4.8 %copy.8 = bf16[32,4,32,512]{3,2,1,0:T(8,128)(2,1)} copy(bf16[32,4,32,512]{3,2,0,1:T(8,128)(2,1)} %get-tuple-element.23) | data formatting | bytes 8388608 | tf_op jit(solution)/shard_map/transpose | solution.py:91
  254.1 2.3 copy.7
  257.1 2.6 copy.10
  260.4 2.7 copy.9
  263.1 35.1 %multiply_convert_fusion = bf16[32,512,2048]{2,1,0:T(8,128)(2,1)} fusion(bf16[32,128,512]{2,1,0:T(8,128)(2,1)} %bitcast.83, bf16[32,128,512]{2,1,0:T(8,128)(2,1)} %bitcast.86, bf16[32,128,512]{2,1,0:T(8,128)(2,1)} %bitcast.87, bf16[32,128,512]{2,1,0:T(8,128)(2,1)} %bitcast.84, bf16[32,128,512]{2,1,0:T(8,128)(2,1)} %bitcast.85), kind=kOutput, calls=%fused_computation | convolution fusion | flops 8724152320 | bytes 88080384 | tf_op jit(solution)/shard_map/dot_general | solution.py:99
  298.2 107.3 %reshape.66 = bf16[32,512,2,1024]{3,2,1,0:T(2,128)(2,1)} reshape(bf16[32,512,2048]{2,1,0:T(8,128)(2,1)} %multiply_convert_fusion) | data formatting | bytes 134217728 | tf_op jit(solution)/shard_map/reshape | solution.py:103
  (112 shorter events, 37.8 us)
Async XLA Ops:
  2.9 15.4 %collective-permute-start.1 = (bf16[15,128,256]{2,1,0:T(8,128)(2,1)S(1)}, bf16[15,128,256]{2,1,0:T(8,128)(2,1)S(1)}, u32[]{:S(2)}, u32[]{:S(2)}) collective-permute-start(bf16[15,128,256]{2,1,0:T(8,128)(2,1)S(1)} %bitcast.109), channel_id=1, source_target_pairs={{0,1},{1,2},{2,3},{4,5},{5,6},{6,7},{8,9},{9,10},{10,11},{12,13},{... | collective-permute-start | bytes 2949128 | tf_op jit(solution)/shard_map/ppermute | solution.py:19
  4.8 24.0 %collective-permute-start = (bf16[15,128,256]{2,1,0:T(8,128)(2,1)S(1)}, bf16[15,128,256]{2,1,0:T(8,128)(2,1)S(1)}, u32[]{:S(2)}, u32[]{:S(2)}) collective-permute-start(bf16[15,128,256]{2,1,0:T(8,128)(2,1)S(1)} %bitcast.108), channel_id=1, source_target_pairs={{0,1},{1,2},{2,3},{4,5},{5,6},{6,7},{8,9},{9,10},{10,11},{12,13},{... | collective-permute-start | bytes 2949128 | tf_op jit(solution)/shard_map/ppermute | solution.py:19
  34.5 77.2 %copy-start.15 = (bf16[8,2,16,512]{3,2,1,0:T(8,128)(2,1)}, bf16[8,2,16,512]{3,2,1,0:T(8,128)(2,1)S(1)}, u32[]{:S(2)}) copy-start(bf16[8,2,16,512]{3,2,1,0:T(8,128)(2,1)S(1)} %get-tuple-element.42) | copy-start | bytes 786436
  34.6 9.0 %collective-permute-start.4 = (bf16[8,32,512]{2,1,0:T(8,128)(2,1)S(1)}, bf16[8,32,512]{2,1,0:T(8,128)(2,1)S(1)}, u32[]{:S(2)}, u32[]{:S(2)}) collective-permute-start(bf16[8,32,512]{2,1,0:T(8,128)(2,1)S(1)} %bitcast.78), channel_id=1, source_target_pairs={{0,2},{1,3},{2,0},{3,1},{4,6},{5,7},{6,4},{7,5},{8,10},{9,11},{10,... | collective-permute-start | bytes 786440 | tf_op jit(solution)/shard_map/ppermute | solution.py:154
  34.6 11.7 %collective-permute-start.2 = (bf16[8,32,512]{2,1,0:T(8,128)(2,1)S(1)}, bf16[8,32,512]{2,1,0:T(8,128)(2,1)S(1)}, u32[]{:S(2)}, u32[]{:S(2)}) collective-permute-start(bf16[8,32,512]{2,1,0:T(8,128)(2,1)S(1)} %bitcast.73), channel_id=1, source_target_pairs={{0,2},{1,3},{2,0},{3,1},{4,6},{5,7},{6,4},{7,5},{8,10},{9,11},{10,... | collective-permute-start | bytes 786440 | tf_op jit(solution)/shard_map/ppermute | solution.py:154
  43.6 2.9 collective-permute-start.5
  46.4 2.8 collective-permute-start.3
  47.6 4.7 %collective-permute-start.13 = (bf16[4,8,32,512]{3,2,1,0:T(8,128)(2,1)}, bf16[4,8,32,512]{3,2,1,0:T(8,128)(2,1)}, u32[]{:S(2)}, u32[]{:S(2)}) collective-permute-start(bf16[4,8,32,512]{3,2,1,0:T(8,128)(2,1)} %pad_maximum_fusion.7), channel_id=1, source_target_pairs={{0,8},{4,12},{9,17},{13,21},{18,10},{22,14},{27,19},{31,23}} | collective-permute-start | bytes 3145736 | tf_op jit(solution)/shard_map/ppermute | solution.py:159
  50.4 4.5 %collective-permute-start.8 = (bf16[4,8,32,512]{3,2,1,0:T(8,128)(2,1)}, bf16[4,8,32,512]{3,2,1,0:T(8,128)(2,1)}, u32[]{:S(2)}, u32[]{:S(2)}) collective-permute-start(bf16[4,8,32,512]{3,2,1,0:T(8,128)(2,1)} %pad_maximum_fusion.6), channel_id=1, source_target_pairs={{0,8},{4,12},{9,17},{13,21},{18,10},{22,14},{27,19},{31,23}} | collective-permute-start | bytes 3145736 | tf_op jit(solution)/shard_map/ppermute | solution.py:159
  53.6 30.2 %copy-start.8 = (bf16[4,8,32,512]{3,2,1,0:T(8,128)(2,1)}, bf16[4,8,32,512]{3,2,1,0:T(8,128)(2,1)S(1)}, u32[]{:S(2)}) copy-start(bf16[4,8,32,512]{3,2,1,0:T(8,128)(2,1)S(1)} %broadcast_select_fusion.10) | copy-start | bytes 3145732
  53.6 28.1 %collective-permute-start.14 = (bf16[4,8,32,512]{3,2,1,0:T(8,128)(2,1)S(1)}, bf16[4,8,32,512]{3,2,1,0:T(8,128)(2,1)}, u32[]{:S(2)}, u32[]{:S(2)}) collective-permute-start(bf16[4,8,32,512]{3,2,1,0:T(8,128)(2,1)S(1)} %broadcast_select_fusion.10), channel_id=1, source_target_pairs={{8,16},{12,20},{17,25},{21,29},{9,1},{13,5},{10,2},{14,6},{18,26},... | collective-permute-start | bytes 3145736 | tf_op jit(solution)/shard_map/ppermute | solution.py:163
  57.3 52.8 %collective-permute-start.9 = (bf16[4,8,32,512]{3,2,1,0:T(8,128)(2,1)S(1)}, bf16[4,8,32,512]{3,2,1,0:T(8,128)(2,1)}, u32[]{:S(2)}, u32[]{:S(2)}) collective-permute-start(bf16[4,8,32,512]{3,2,1,0:T(8,128)(2,1)S(1)} %broadcast_select_fusion.11), channel_id=1, source_target_pairs={{8,16},{12,20},{17,25},{21,29},{9,1},{13,5},{10,2},{14,6},{18,26},... | collective-permute-start | bytes 3145736 | tf_op jit(solution)/shard_map/ppermute | solution.py:163
  58.6 25.2 %collective-permute-start.6 = (bf16[8,32,512]{2,1,0:T(8,128)(2,1)S(1)}, bf16[8,32,512]{2,1,0:T(8,128)(2,1)S(1)}, u32[]{:S(2)}, u32[]{:S(2)}) collective-permute-start(bf16[8,32,512]{2,1,0:T(8,128)(2,1)S(1)} %bitcast.99), channel_id=1, source_target_pairs={{0,2},{1,3},{2,0},{3,1},{4,6},{5,7},{6,4},{7,5},{8,10},{9,11},{10,... | collective-permute-start | bytes 786440 | tf_op jit(solution)/shard_map/ppermute | solution.py:154
  79.4 32.3 %collective-permute-start.11 = (bf16[8,32,512]{2,1,0:T(8,128)(2,1)S(1)}, bf16[8,32,512]{2,1,0:T(8,128)(2,1)S(1)}, u32[]{:S(2)}, u32[]{:S(2)}) collective-permute-start(bf16[8,32,512]{2,1,0:T(8,128)(2,1)S(1)} %bitcast.96), channel_id=1, source_target_pairs={{0,2},{1,3},{2,0},{3,1},{4,6},{5,7},{6,4},{7,5},{8,10},{9,11},{10,... | collective-permute-start | bytes 786440 | tf_op jit(solution)/shard_map/ppermute | solution.py:154
  81.7 34.4 %collective-permute-start.15 = (bf16[4,8,32,512]{3,2,1,0:T(8,128)(2,1)}, bf16[4,8,32,512]{3,2,1,0:T(8,128)(2,1)}, u32[]{:S(2)}, u32[]{:S(2)}) collective-permute-start(bf16[4,8,32,512]{3,2,1,0:T(8,128)(2,1)} %collective-permute-done.14), channel_id=1, source_target_pairs={{16,24},{20,28},{11,3},{15,7}} | collective-permute-start | bytes 3145736 | tf_op jit(solution)/shard_map/ppermute | solution.py:165
  83.8 28.8 %collective-permute-start.7 = (bf16[2,8,32,512]{3,2,1,0:T(8,128)(2,1)S(1)}, bf16[2,8,32,512]{3,2,1,0:T(8,128)(2,1)}, u32[]{:S(2)}, u32[]{:S(2)}) collective-permute-start(bf16[2,8,32,512]{3,2,1,0:T(8,128)(2,1)S(1)} %pad_maximum_fusion.12), channel_id=1, source_target_pairs={{0,1},{1,0},{2,3},{3,2},{4,5},{5,4},{6,7},{7,6},{8,9},{9,8},{10,11... | collective-permute-start | bytes 1572872 | tf_op jit(solution)/shard_map/ppermute | solution.py:156
  110.1 8.8 %collective-permute-start.10 = (bf16[4,8,32,512]{3,2,1,0:T(8,128)(2,1)}, bf16[4,8,32,512]{3,2,1,0:T(8,128)(2,1)}, u32[]{:S(2)}, u32[]{:S(2)}) collective-permute-start(bf16[4,8,32,512]{3,2,1,0:T(8,128)(2,1)} %collective-permute-done.9), channel_id=1, source_target_pairs={{16,24},{20,28},{11,3},{15,7}} | collective-permute-start | bytes 3145736 | tf_op jit(solution)/shard_map/ppermute | solution.py:165
  112.6 2.3 collective-permute-start.12
  117.6 26.1 %collective-permute-start.19 = (bf16[4,8,32,512]{3,2,1,0:T(8,128)(2,1)S(1)}, bf16[4,8,32,512]{3,2,1,0:T(8,128)(2,1)S(1)}, u32[]{:S(2)}, u32[]{:S(2)}) collective-permute-start(bf16[4,8,32,512]{3,2,1,0:T(8,128)(2,1)S(1)} %select_select_fusion.2), channel_id=1, source_target_pairs={{0,4},{1,5},{2,6},{3,7},{4,0},{5,1},{6,2},{7,3},{8,12},{9,13},{10,... | collective-permute-start | bytes 3145736 | tf_op jit(solution)/shard_map/ppermute | solution.py:168
  118.2 4.5 %collective-permute-start.18 = (bf16[4,8,32,512]{3,2,1,0:T(8,128)(2,1)S(1)}, bf16[4,8,32,512]{3,2,1,0:T(8,128)(2,1)S(1)}, u32[]{:S(2)}, u32[]{:S(2)}) collective-permute-start(bf16[4,8,32,512]{3,2,1,0:T(8,128)(2,1)S(1)} %pad_maximum_fusion.9), channel_id=1, source_target_pairs={{0,8},{4,12},{9,17},{13,21},{18,10},{22,14},{27,19},{31,23}} | collective-permute-start | bytes 3145736 | tf_op jit(solution)/shard_map/ppermute | solution.py:159
  120.3 24.8 %copy-start.4 = (bf16[4,8,32,512]{3,2,1,0:T(8,128)(2,1)}, bf16[4,8,32,512]{3,2,1,0:T(8,128)(2,1)S(1)}, u32[]{:S(2)}) copy-start(bf16[4,8,32,512]{3,2,1,0:T(8,128)(2,1)S(1)} %select_select_fusion.3) | copy-start | bytes 3145732
  120.3 24.7 %collective-permute-start.16 = (bf16[4,8,32,512]{3,2,1,0:T(8,128)(2,1)S(1)}, bf16[4,8,32,512]{3,2,1,0:T(8,128)(2,1)S(1)}, u32[]{:S(2)}, u32[]{:S(2)}) collective-permute-start(bf16[4,8,32,512]{3,2,1,0:T(8,128)(2,1)S(1)} %pad_maximum_fusion.8), channel_id=1, source_target_pairs={{0,8},{4,12},{9,17},{13,21},{18,10},{22,14},{27,19},{31,23}} | collective-permute-start | bytes 3145736 | tf_op jit(solution)/shard_map/ppermute | solution.py:159
  121.1 44.3 %collective-permute-start.17 = (bf16[4,8,32,512]{3,2,1,0:T(8,128)(2,1)S(1)}, bf16[4,8,32,512]{3,2,1,0:T(8,128)(2,1)S(1)}, u32[]{:S(2)}, u32[]{:S(2)}) collective-permute-start(bf16[4,8,32,512]{3,2,1,0:T(8,128)(2,1)S(1)} %select_select_fusion.3), channel_id=1, source_target_pairs={{0,4},{1,5},{2,6},{3,7},{4,0},{5,1},{6,2},{7,3},{8,12},{9,13},{10,... | collective-permute-start | bytes 3145736 | tf_op jit(solution)/shard_map/ppermute | solution.py:168
  122.8 70.4 %copy-start.12 = (bf16[4,8,32,512]{3,2,1,0:T(8,128)(2,1)}, bf16[4,8,32,512]{3,2,1,0:T(8,128)(2,1)S(1)}, u32[]{:S(2)}) copy-start(bf16[4,8,32,512]{3,2,1,0:T(8,128)(2,1)S(1)} %broadcast_select_fusion.8) | copy-start | bytes 3145732
  143.7 49.5 %copy-start.17 = (bf16[4,8,32,512]{3,2,1,0:T(8,128)(2,1)}, bf16[4,8,32,512]{3,2,1,0:T(8,128)(2,1)S(1)}, u32[]{:S(2)}) copy-start(bf16[4,8,32,512]{3,2,1,0:T(8,128)(2,1)S(1)} %collective-permute-done.19) | copy-start | bytes 3145732
  143.7 23.0 %collective-permute-start.23 = (bf16[4,8,32,512]{3,2,1,0:T(8,128)(2,1)S(1)}, bf16[4,8,32,512]{3,2,1,0:T(8,128)(2,1)}, u32[]{:S(2)}, u32[]{:S(2)}) collective-permute-start(bf16[4,8,32,512]{3,2,1,0:T(8,128)(2,1)S(1)} %broadcast_select_fusion.8), channel_id=1, source_target_pairs={{8,16},{12,20},{17,25},{21,29},{9,1},{13,5},{10,2},{14,6},{18,26},... | collective-permute-start | bytes 3145736 | tf_op jit(solution)/shard_map/ppermute | solution.py:163
  165.4 27.8 %copy-start.19 = (bf16[4,8,32,512]{3,2,1,0:T(8,128)(2,1)}, bf16[4,8,32,512]{3,2,1,0:T(8,128)(2,1)S(1)}, u32[]{:S(2)}) copy-start(bf16[4,8,32,512]{3,2,1,0:T(8,128)(2,1)S(1)} %collective-permute-done.17) | copy-start | bytes 3145732
  165.4 27.8 %collective-permute-start.20 = (bf16[4,8,32,512]{3,2,1,0:T(8,128)(2,1)S(1)}, bf16[4,8,32,512]{3,2,1,0:T(8,128)(2,1)}, u32[]{:S(2)}, u32[]{:S(2)}) collective-permute-start(bf16[4,8,32,512]{3,2,1,0:T(8,128)(2,1)S(1)} %broadcast_select_fusion.9), channel_id=1, source_target_pairs={{8,16},{12,20},{17,25},{21,29},{9,1},{13,5},{10,2},{14,6},{18,26},... | collective-permute-start | bytes 3145736 | tf_op jit(solution)/shard_map/ppermute | solution.py:163
  166.7 28.3 %collective-permute-start.24 = (bf16[4,8,32,512]{3,2,1,0:T(8,128)(2,1)}, bf16[4,8,32,512]{3,2,1,0:T(8,128)(2,1)}, u32[]{:S(2)}, u32[]{:S(2)}) collective-permute-start(bf16[4,8,32,512]{3,2,1,0:T(8,128)(2,1)} %collective-permute-done.23), channel_id=1, source_target_pairs={{16,24},{20,28},{11,3},{15,7}} | collective-permute-start | bytes 3145736 | tf_op jit(solution)/shard_map/ppermute | solution.py:165
  193.2 3.8 collective-permute-start.21
  196.4 26.2 %collective-permute-start.25 = (bf16[4,8,32,512]{3,2,1,0:T(8,128)(2,1)S(1)}, bf16[4,8,32,512]{3,2,1,0:T(8,128)(2,1)S(1)}, u32[]{:S(2)}, u32[]{:S(2)}) collective-permute-start(bf16[4,8,32,512]{3,2,1,0:T(8,128)(2,1)S(1)} %select_select_fusion), channel_id=1, source_target_pairs={{0,4},{1,5},{2,6},{3,7},{4,0},{5,1},{6,2},{7,3},{8,12},{9,13},{10,... | collective-permute-start | bytes 3145736 | tf_op jit(solution)/shard_map/ppermute | solution.py:168
  198.5 44.1 %collective-permute-start.22 = (bf16[4,8,32,512]{3,2,1,0:T(8,128)(2,1)S(1)}, bf16[4,8,32,512]{3,2,1,0:T(8,128)(2,1)S(1)}, u32[]{:S(2)}, u32[]{:S(2)}) collective-permute-start(bf16[4,8,32,512]{3,2,1,0:T(8,128)(2,1)S(1)} %select_select_fusion.1), channel_id=1, source_target_pairs={{0,4},{1,5},{2,6},{3,7},{4,0},{5,1},{6,2},{7,3},{8,12},{9,13},{10,... | collective-permute-start | bytes 3145736 | tf_op jit(solution)/shard_map/ppermute | solution.py:168
  (17 other events, 70.8 us)
